TPU v7x, 32 devices: a whole 2x2x4 slice. The times are simulated.
32 devices in a mesh: row: 8 (over z, y), col: 4 (over x, core).
Axes of the slice: x: 2, y: 2, z: 4, core: 2. Of those that a mesh axis runs over, the one named last changes fastest.
Arguments:
- amplitudes: float32 [16, 16, 400, 400], P('row', None, 'col'), may hold values from -6 to 6
- integrals: float32 [32, 32, 400, 400], P('row', None, 'col'), may hold values from -0.015625 to 0.015625
- rest: float32 [16, 16, 32, 32], P('col', None, 'row'), may hold values from -6 to 6
- occ_energy: float32 [16], replicated, may hold values from -2 to -0.5
- vir_energy: float32 [32], replicated, may hold values from 0.5 to 3
Outputs:
- new_amps: float32 [16, 16, 32, 32], P('col', None, 'row')
All inputs are finite; a program needn't handle non-finite values.
Results may differ from a plain program's by a relative error of at most 0.000057.
Values sent between devices are 32-bit elements; how exact they have to be, the bound alone decides.
A program may use at most 128 MiB of HBM per device.

v0:
```python
import jax
import jax.numpy as jnp
from jax import lax
from jax.sharding import PartitionSpec as P


def on_device(amplitudes, integrals, rest, occ_energy, vir_energy):
    row_index = lax.axis_index("row")
    col_index = lax.axis_index("col")
    a_count = integrals.shape[0]
    b_count = integrals.shape[1]
    integral_slab = integrals.reshape(a_count * b_count, -1)
    occupied = amplitudes.shape[1]
    shard_piece = lax.all_gather(amplitudes, "row", axis=0, tiled=True)
    piece_rows = shard_piece.shape[0]
    flattened = shard_piece.reshape(piece_rows * occupied, -1)
    product = lax.dot_general(
        flattened,
        integral_slab,
        (((1,), (1,)), ((), ())),
        precision=lax.Precision.HIGHEST,
        preferred_element_type=jnp.float32,
    )
    partial_value = product.reshape(piece_rows, occupied, a_count, b_count)
    summed = lax.psum_scatter(partial_value, "col", scatter_dimension=0, tiled=True)
    moved = lax.all_to_all(
        lax.all_to_all(summed, "row", split_axis=3, concat_axis=2, tiled=True),
        "col",
        split_axis=1,
        concat_axis=0,
        tiled=True,
    )
    combined = summed + jnp.transpose(moved, (1, 0, 3, 2))
    i_count = combined.shape[0]
    occ_local = lax.dynamic_slice_in_dim(occ_energy, col_index * i_count, i_count, 0)
    vir_local = lax.dynamic_slice_in_dim(vir_energy, row_index * a_count, a_count, 0)
    denominator = (
        vir_local[None, None, :, None]
        + vir_energy[None, None, None, :]
        - occ_local[:, None, None, None]
        - occ_energy[None, :, None, None]
    )
    return (combined + rest) / denominator


def solution(mesh):
    in_specs = (
        P("row", None, "col", None),
        P("row", None, "col", None),
        P("col", None, "row", None),
        P(),
        P(),
    )
    out_specs = P("col", None, "row", None)
    return jax.shard_map(
        on_device, mesh=mesh, in_specs=in_specs, out_specs=out_specs, check_vma=False
    )
```

profile of v0, /device:TPU:0, one launch (start us, length us, event | category | flops | bytes accessed | tf_op | source)
XLA Modules:
  0.0 1146.0 jit_solution(209215597239541560)
XLA Ops:
  6.5 0.0 all-gather.2.cloned.1.call-start
  6.5 0.7 all-gather.2.cloned.1.call-update
  7.3 0.0 copy-start.2
  7.3 0.0 copy-start.1
  7.3 0.0 copy-start
  7.3 0.0 reduce-scatter.2.cloned.1.call-start
  7.3 995.9 %all-gather.2.cloned.1.call-done = f32[16,16,100,400]{3,1,2,0:T(8,128)} async-done(((f32[2,16,100,400]{3,1,2,0:T(8,128)}), f32[16,16,100,400]{3,1,2,0:T(8,128)}) %all-gather.2.cloned.1.call-update) | async-done | bytes 40960016 | tf_op jit(solution)/shard_map/all_gather | solution.py:14
  1003.3 87.4 %fusion.3 = f32[16,16,4,32]{3,1,2,0:T(8,128)} fusion(f32[4,32,100,400]{3,1,2,0:T(8,128)} %param.6, f32[16,16,100,400]{3,1,2,0:T(8,128)} %all-gather.2.cloned.1.call-done), kind=kOutput, calls=%fused_computation.3 | convolution fusion | flops 15728640000 | bytes 61571072 | tf_op jit(solution)/shard_map/dot_general | solution.py:17
  1090.7 0.0 reduce-scatter.2.cloned.1.call-update
  1090.7 0.0 copy-done.2
  1090.8 0.1 dynamic_slice.6
  1090.8 21.7 %reduce-scatter.2.cloned.1.call-done = f32[4,16,4,32]{3,1,2,0:T(8,128)} async-done(((f32[16,16,4,32]{3,1,2,0:T(8,128)}), f32[4,16,4,32]{3,1,2,0:T(8,128)}) %reduce-scatter.2.cloned.1.call-update) | async-done | bytes 32784 | tf_op jit(solution)/shard_map/reduce_scatter | solution.py:25
  1112.5 1.1 copy.14
  1113.6 0.8 reshape.50
  1114.4 5.5 all-to-all-start
  1119.9 0.1 broadcast_add_fusion
  1120.0 0.0 copy-done.1
  1120.0 0.1 dynamic_slice.7
  1120.1 6.5 all-to-all-done
  1126.6 0.5 broadcast.37
  1127.2 0.7 reduce
  1127.9 0.2 reshape.51
  1128.1 0.1 copy.15
  1128.2 0.2 copy.16
  1128.4 0.1 copy.17
  1128.5 0.8 reshape.52
  1129.3 3.3 all-to-all-start.1
  1132.5 0.1 broadcast_subtract_fusion
  1132.6 3.8 all-to-all-done.1
  1136.5 0.7 reduce.1
  1137.2 0.1 reshape.53
  1137.4 0.1 copy.19
  1137.5 0.0 copy-done
  1137.5 1.0 fusion.8
  1138.5 0.7 copy.21
  (1 shorter events, 0.0 us)
Async XLA Ops:
  6.5 996.7 %all-gather.2.cloned.1.call-start = ((), (), s32[]{:S(2)}) async-start(), calls=%async_computation.3 | async-start | bytes 58982400 | tf_op jit(solution)/shard_map/all_gather | solution.py:14
  7.3 1083.5 %copy-start.2 = (f32[32]{0:T(128)S(1)}, f32[32]{0:T(128)}, u32[]{:S(2)}) copy-start(f32[32]{0:T(128)} %param.9) | copy-start | bytes 388
  7.3 1112.7 %copy-start.1 = (f32[16]{0:T(128)S(1)}, f32[16]{0:T(128)}, u32[]{:S(2)}) copy-start(f32[16]{0:T(128)} %param.8) | copy-start | bytes 196
  7.3 1130.2 %copy-start = (f32[4,16,4,32]{3,2,1,0:T(4,128)S(1)}, f32[4,16,4,32]{3,2,1,0:T(4,128)}, u32[]{:S(2)}) copy-start(f32[4,16,4,32]{3,2,1,0:T(4,128)} %param.7) | copy-start | bytes 98308
  7.3 1105.2 %reduce-scatter.2.cloned.1.call-start = ((), (), s32[]{:S(2)}) async-start(), calls=%async_computation.4 | async-start | bytes 655360 | tf_op jit(solution)/shard_map/reduce_scatter | solution.py:25
  1114.4 12.2 %all-to-all-start = ((f32[8,1,1024]{2,1,0:T(1,128)}), f32[8,1,1024]{2,1,0:T(1,128)S(1)}, u32[]{:S(2)}, u32[]{:S(2)}) async-start(f32[8,1,1024]{2,1,0:T(1,128)} %reshape.50), calls=%async_computation.1 | async-start | bytes 65536 | tf_op jit(solution)/shard_map/all_to_all | solution.py:27
  1129.3 7.2 all-to-all-start.1
Sparse Core Ops, SparseCore 0:
  8.9 994.3 all-gather.1
  1090.9 21.6 reduce-scatter.1
where the time goes:
time: 1150 us
  waiting for transfers between devices  1030 us (90%)
  matrix products  87.4 us (8%)
  between operations  13.5 us (1%)
    all_gather x1, waiting for transfers between devices, on_device(): shard_piece = lax.all_gather(amplitudes, 'row', axis=0, tiled=True)  996 us
    dot_general x1, matrix products, on_device(): lax.dot_general(flattened, integral_slab, (((1,), (1,)), ((), ())), preci...  87.4 us
  transfers between devices with their start and end apart: 4, of which 4 were waited for; matrix products, arithmetic and copies ran while one was open for 0% of the time, Pallas kernels for 0%

commit v1 on v0

v1 whole, which is shorter than its diff:
```python
import functools

import jax
import jax.numpy as jnp
from jax import lax
from jax.experimental import pallas as pl
from jax.experimental.pallas import tpu as pltpu
from jax.sharding import PartitionSpec as P

MESH = pl.DeviceIdType.MESH
LANES = 128
LAG = 2


def chunk_of(count):
    return max(k for k in range(1, 11) if count % k == 0)


def split(x):
    high = x.astype(jnp.bfloat16)
    return high, (x - high.astype(jnp.float32)).astype(jnp.bfloat16)


def ring_kernel(n, cc, t_ref, ttail_ref, v_ref, vtail_ref, out_ref, held, vbuf, acc,
                load_sem, v_sem, send_sem, recv_sem):
    occ_rows, c_count, j_count, _ = t_ref.shape
    a_count, _, b_count, _ = v_ref.shape
    tail_tiles = ttail_ref.shape[0]
    full = v_ref.shape[3] // LANES
    rows = n * occ_rows * j_count
    cols = a_count * b_count
    mains = c_count // cc
    chunks = mains + 1

    row = lax.axis_index("row")
    half = n // 2

    def row_at(position):
        upper = lax.div(position, half)
        return (1 - upper) * (2 * position) + upper * (2 * (n - 1 - position) + 1)

    odd = lax.rem(row, 2)
    place = (1 - odd) * lax.div(row, 2) + odd * (n - 1 - lax.div(row, 2))
    source = {step: row_at(lax.rem(place + step + n, n)) for step in range(-half, half + 1)}

    def tiles(q):
        if q < mains:
            return pl.ds(q * full * cc, full * cc)
        return pl.ds(mains * full * cc, tail_tiles)

    def own_loads(q):
        if q == mains:
            return [pltpu.make_async_copy(ttail_ref, held.at[row, tiles(q)], load_sem.at[q])]
        return [
            pltpu.make_async_copy(
                t_ref.at[i, pl.ds(q * cc, cc), :, pl.ds(part * LANES, LANES)],
                held.at[row, pl.ds(q * full * cc + part * cc, cc), pl.ds(i * j_count, j_count), :],
                load_sem.at[q],
            )
            for i in range(occ_rows)
            for part in range(full)
        ]

    def v_load(q):
        return pltpu.make_async_copy(v_ref.at[:, pl.ds(q * cc, cc)], vbuf.at[q % 2], v_sem.at[q % 2])

    def hops(q, way):
        return half if (q + way) % 2 == 0 else n - 1 - half

    def send(q, step, way):
        sign = 1 if way == 0 else -1
        data = held.at[source[-sign * (step - 1)], tiles(q)]
        return pltpu.make_async_remote_copy(
            src_ref=data, dst_ref=data,
            send_sem=send_sem.at[q, step - 1, way], recv_sem=recv_sem.at[q, step - 1, way],
            device_id={"row": source[sign]}, device_id_type=MESH,
        )

    def arrival(q, step, way):
        sign = 1 if way == 0 else -1
        data = held.at[source[-sign * step], tiles(q)]
        return pltpu.make_async_remote_copy(
            src_ref=data, dst_ref=data,
            send_sem=send_sem.at[q, step - 1, way], recv_sem=recv_sem.at[q, step - 1, way],
            device_id={"row": source[sign]}, device_id_type=MESH,
        )

    def add_product(t, v):
        t_high, t_low = split(t)
        v_high, v_low = split(v)
        dims = (((1,), (1,)), ((), ()))
        both = lax.dot_general(t_high, jnp.concatenate([v_high, v_low], axis=0), dims,
                               preferred_element_type=jnp.float32)
        rest = lax.dot_general(t_low, v_high, dims, preferred_element_type=jnp.float32)
        acc[...] += both[:, :cols] + both[:, cols:] + rest

    def compute(q):
        if q == mains:
            @pl.loop(0, tail_tiles)
            def _(k):
                add_product(held[:, mains * full * cc + k].reshape(rows, LANES), vtail_ref[k])
            return
        v_load(q).wait()

        @pl.loop(0, cc)
        def _(k):
            t = jnp.concatenate(
                [held[:, q * full * cc + part * cc + k].reshape(rows, LANES) for part in range(full)], axis=1)
            v = vbuf[q % 2, :, k, :, : full * LANES].reshape(cols, full * LANES)
            add_product(t, v)
        if q + 2 < mains:
            v_load(q + 2).start()

    for q in range(chunks):
        for copy in own_loads(q):
            copy.start()
    for q in range(min(2, mains)):
        v_load(q).start()
    acc[...] = jnp.zeros_like(acc)

    barrier = pltpu.get_barrier_semaphore()
    for step in (-1, 1):
        pl.semaphore_signal(barrier, inc=1, device_id={"row": source[step]}, device_id_type=MESH)
    pl.semaphore_wait(barrier, 2)

    for turn in range(chunks + LAG * half):
        for step in range(1, half + 2):
            q = turn - LAG * (step - 1)
            if not 0 <= q < chunks:
                continue
            if step == 1:
                whole = held.at[row, tiles(q)]
                pltpu.make_async_copy(whole, whole, load_sem.at[q]).wait()
            for way in range(2):
                if step > 1 and step - 1 <= hops(q, way):
                    arrival(q, step - 1, way).wait_recv()
                if step <= hops(q, way):
                    send(q, step, way).start()
            if step == half + 1:
                compute(q)
    for q in range(chunks):
        for way in range(2):
            for step in range(1, hops(q, way) + 1):
                send(q, step, way).wait_send()
    out_ref[...] = acc[...]


def packed_tail(x, start):
    c_count, rows, d_count = x.shape
    width = d_count - start
    per = LANES // width
    groups = -(-c_count // per)
    cut = jnp.pad(x[:, :, start:], ((0, groups * per - c_count), (0, 0), (0, 0)))
    cut = cut.reshape(groups, per, rows, width).transpose(0, 2, 1, 3).reshape(groups, rows, per * width)
    return jnp.pad(cut, ((0, 0), (0, 0), (0, LANES - per * width)))


def partial_ladder(n, amplitudes, integrals):
    occ_rows, j_count, c_count, d_count = amplitudes.shape
    a_count, b_count = integrals.shape[:2]
    full = d_count // LANES
    t = jnp.transpose(amplitudes, (0, 2, 1, 3))
    v = jnp.transpose(integrals, (0, 2, 1, 3))
    t_tail = packed_tail(
        jnp.transpose(t[..., full * LANES:], (1, 0, 2, 3)).reshape(c_count, occ_rows * j_count, -1), 0)
    v_tail = packed_tail(
        jnp.transpose(v[..., full * LANES:], (1, 0, 2, 3)).reshape(c_count, a_count * b_count, -1), 0)
    cc = chunk_of(c_count)
    chunks = c_count // cc + 1
    tiles = c_count * full + t_tail.shape[0]
    rows, cols = n * occ_rows * j_count, a_count * b_count
    half = n // 2
    return pl.pallas_call(
        functools.partial(ring_kernel, n, cc),
        out_shape=jax.ShapeDtypeStruct((rows, cols), jnp.float32),
        in_specs=[pl.BlockSpec(memory_space=pl.ANY)] * 3 + [pl.BlockSpec(memory_space=pltpu.VMEM)],
        out_specs=pl.BlockSpec(memory_space=pltpu.VMEM),
        scratch_shapes=[
            pltpu.VMEM((n, tiles, occ_rows * j_count, LANES), jnp.float32),
            pltpu.VMEM((2, a_count, cc, b_count, d_count), jnp.float32),
            pltpu.VMEM((rows, cols), jnp.float32),
            pltpu.SemaphoreType.DMA((chunks,)),
            pltpu.SemaphoreType.DMA((2,)),
            pltpu.SemaphoreType.DMA((chunks, half, 2)),
            pltpu.SemaphoreType.DMA((chunks, half, 2)),
        ],
        compiler_params=pltpu.CompilerParams(
            collective_id=0, has_side_effects=True, vmem_limit_bytes=58 * 2**20),
        cost_estimate=pl.CostEstimate(
            flops=6 * rows * cols * c_count * d_count,
            bytes_accessed=4 * c_count * d_count * (rows + cols), transcendentals=0),
    )(t, t_tail, v, v_tail)


def on_device(n, amplitudes, integrals, rest, occ_energy, vir_energy):
    row_index = lax.axis_index("row")
    col_index = lax.axis_index("col")
    a_count = integrals.shape[0]
    b_count = integrals.shape[1]
    occupied = amplitudes.shape[1]
    partial_value = partial_ladder(n, amplitudes, integrals).reshape(
        n * amplitudes.shape[0], occupied, a_count, b_count)
    summed = lax.psum_scatter(partial_value, "col", scatter_dimension=0, tiled=True)
    moved = lax.all_to_all(
        lax.all_to_all(summed, "row", split_axis=3, concat_axis=2, tiled=True),
        "col",
        split_axis=1,
        concat_axis=0,
        tiled=True,
    )
    combined = summed + jnp.transpose(moved, (1, 0, 3, 2))
    i_count = combined.shape[0]
    occ_local = lax.dynamic_slice_in_dim(occ_energy, col_index * i_count, i_count, 0)
    vir_local = lax.dynamic_slice_in_dim(vir_energy, row_index * a_count, a_count, 0)
    denominator = (
        vir_local[None, None, :, None]
        + vir_energy[None, None, None, :]
        - occ_local[:, None, None, None]
        - occ_energy[None, :, None, None]
    )
    return (combined + rest) / denominator


def solution(mesh):
    in_specs = (
        P("row", None, "col", None),
        P("row", None, "col", None),
        P("col", None, "row", None),
        P(),
        P(),
    )
    out_specs = P("col", None, "row", None)
    return jax.shard_map(
        functools.partial(on_device, mesh.shape["row"]), mesh=mesh, in_specs=in_specs, out_specs=out_specs,
        check_vma=False
    )
```

time: 1150 us -> 483 us (0.42)
  waiting for transfers between devices: 1030 us -> 32.3 us
  Pallas kernels: 0 us -> 401 us
  matrix products: 87.4 us -> 0 us
  local copies, waits for them, and re-layouts: 4.95 us -> 24.6 us
    all_gather x1 -> x0, waiting for transfers between devices: 996 us -> none  [on_device(): shard_piece = lax.all_gather(amplitudes, 'row', axis=0, tiled=True)]
    pallas_call x0 -> x1, Pallas kernels: none -> 401 us  [partial_ladder(): pl.pallas_call(functools.partial(ring_kernel, n, cc), out_shape=jax.Shape...]
    dot_general x1 -> x0, matrix products: 87.4 us -> none  [on_device(): lax.dot_general(flattened, integral_slab, (((1,), (1,)), ((), ())), preci...]
    transpose x0 -> x4, local copies, waits for them, and re-layouts: none -> 14.2 us  [the longest x2 12 us: partial_ladder(): jnp.transpose(v[..., full * LANES:], (1, 0, 2, 3))]
  transfers between devices with their start and end apart: 4 -> 3, of which waited for: 4 -> 3; matrix products, arithmetic and copies ran while one was open for 0% -> 0% of each run, Pallas kernels for 0% -> 0%
where the time goes in v1:
time: 483 us
  Pallas kernels  401 us (83%)
  waiting for transfers between devices  32.3 us (7%)
  local copies, waits for them, and re-layouts  24.6 us (5%)
  between operations  13.5 us (3%)
  starting transfers between devices  8.78 us (2%)
    pallas_call x1, Pallas kernels, partial_ladder(): pl.pallas_call(functools.partial(ring_kernel, n, cc), out_shape=jax.Shape...  401 us
    reduce_scatter x1, waiting for transfers between devices, on_device(): lax.psum_scatter(partial_value, 'col', scatter_dimension=0, tiled=True)  21.9 us
    transpose x2, local copies, waits for them, and re-layouts, partial_ladder(): jnp.transpose(v[..., full * LANES:], (1, 0, 2, 3))  12 us
  transfers between devices with their start and end apart: 3, of which 3 were waited for; matrix products, arithmetic and copies ran while one was open for 0% of the time, Pallas kernels for 0%

profile of v1, /device:TPU:0, one launch (start us, length us, event | category | flops | bytes accessed | tf_op | source)
XLA Modules:
  0.0 483.0 jit_solution(2612340158358742576)
XLA Ops:
  6.5 0.0 reduce-scatter.2.cloned.1.call-start
  6.5 6.3 %slice_bitcast_fusion = f32[100,4,32,16]{3,2,0,1:T(8,128)} fusion(f32[4,100,32,400]{3,2,1,0:T(8,128)} %bitcast.32), kind=kLoop, calls=%fused_computation | loop fusion | bytes 1638400 | tf_op jit(solution)/shard_map/transpose | solution.py:167
  12.9 5.7 %copy.33 = f32[100,4,32,16]{0,3,2,1:T(8,128)S(1)} copy(f32[100,4,32,16]{3,2,0,1:T(8,128)} %slice_bitcast_fusion) | data formatting | bytes 1638400 | tf_op jit(solution)/shard_map/transpose | solution.py:167
  18.6 0.7 copy.47
  19.2 0.1 pad.9.clone
  19.3 1.2 copy.36.vtail_ref
  20.5 1.5 slice_bitcast_fusion.1
  22.1 0.7 copy.31
  22.7 0.5 copy.46
  23.2 0.1 pad.8.clone
  23.2 1.0 copy.35.ttail_ref
  24.2 0.0 copy-start.2
  24.2 0.0 copy-start.1
  24.2 0.0 copy-start
  24.2 401.3 %shard_map.55 = f32[256,128]{1,0:T(8,128)} custom-call(f32[2,100,16,400]{3,2,1,0:T(8,128)} %bitcast.35, f32[13,32,128]{2,1,0:T(8,128)} %copy.35.ttail_ref, f32[4,100,32,400]{3,2,1,0:T(8,128)} %bitcast.33, f32[13,128,128]{2,1,0:T(8,128)} %copy.36.vtail_ref), custom_call_target="tpu_custom_call" | custom-call | flops 7864320000 | bytes 61440000 | tf_op jit(solution)/shard_map/pallas_call | solution.py:173
  425.5 1.2 reshape.67
  426.7 0.8 copy.37
  427.5 0.0 reduce-scatter.2.cloned.1.call-update
  427.5 0.0 copy-done.2
  427.5 0.1 dynamic_slice.6
  427.6 21.9 %reduce-scatter.2.cloned.1.call-done = f32[4,16,4,32]{3,1,2,0:T(8,128)} async-done(((f32[16,16,4,32]{3,1,2,0:T(8,128)}), f32[4,16,4,32]{3,1,2,0:T(8,128)}) %reduce-scatter.2.cloned.1.call-update) | async-done | bytes 32784 | tf_op jit(solution)/shard_map/reduce_scatter | solution.py:203
  449.5 1.1 copy.38
  450.6 0.8 reshape.68
  451.4 5.5 %all-to-all-start = ((f32[8,1,1024]{2,1,0:T(1,128)}), f32[8,1,1024]{2,1,0:T(1,128)S(1)}, u32[]{:S(2)}, u32[]{:S(2)}) async-start(f32[8,1,1024]{2,1,0:T(1,128)} %reshape.68), calls=%async_computation.1 | async-start | bytes 65536 | tf_op jit(solution)/shard_map/all_to_all | solution.py:205
  456.9 0.1 broadcast_add_fusion
  457.0 0.0 copy-done.1
  457.0 0.1 dynamic_slice.7
  457.1 6.5 %all-to-all-done = f32[8,1,1024]{2,1,0:T(1,128)S(1)} async-done(((f32[8,1,1024]{2,1,0:T(1,128)}), f32[8,1,1024]{2,1,0:T(1,128)S(1)}, u32[]{:S(2)}, u32[]{:S(2)}) %all-to-all-start) | async-done | bytes 32800 | tf_op jit(solution)/shard_map/all_to_all | solution.py:205
  463.6 0.5 broadcast.41
  464.2 0.7 reduce
  464.9 0.2 reshape.69
  465.1 0.1 copy.39
  465.2 0.2 copy.40
  465.4 0.1 copy.41
  465.5 0.8 reshape.70
  466.3 3.3 all-to-all-start.1
  469.6 0.1 broadcast_subtract_fusion
  469.6 3.8 all-to-all-done.1
  473.5 0.7 reduce.1
  474.2 0.1 reshape.71
  474.4 0.1 copy.43
  474.5 0.0 copy-done
  474.5 1.0 fusion
  475.5 0.7 copy.45
  (1 shorter events, 0.0 us)
Async XLA Ops:
  6.5 443.0 %reduce-scatter.2.cloned.1.call-start = ((), (), s32[]{:S(2)}) async-start(), calls=%async_computation.3 | async-start | bytes 655360 | tf_op jit(solution)/shard_map/reduce_scatter | solution.py:203
  24.2 403.3 %copy-start.2 = (f32[32]{0:T(128)S(1)}, f32[32]{0:T(128)}, u32[]{:S(2)}) copy-start(f32[32]{0:T(128)} %param.9) | copy-start | bytes 388
  24.2 432.8 %copy-start.1 = (f32[16]{0:T(128)S(1)}, f32[16]{0:T(128)}, u32[]{:S(2)}) copy-start(f32[16]{0:T(128)} %param.8) | copy-start | bytes 196
  24.2 450.3 %copy-start = (f32[4,16,4,32]{3,2,1,0:T(4,128)S(1)}, f32[4,16,4,32]{3,2,1,0:T(4,128)}, u32[]{:S(2)}) copy-start(f32[4,16,4,32]{3,2,1,0:T(4,128)} %param.7) | copy-start | bytes 98308
  451.4 12.2 %all-to-all-start = ((f32[8,1,1024]{2,1,0:T(1,128)}), f32[8,1,1024]{2,1,0:T(1,128)S(1)}, u32[]{:S(2)}, u32[]{:S(2)}) async-start(f32[8,1,1024]{2,1,0:T(1,128)} %reshape.68), calls=%async_computation.1 | async-start | bytes 65536 | tf_op jit(solution)/shard_map/all_to_all | solution.py:205
  466.3 7.2 %all-to-all-start.1 = ((f32[4,1,2048]{2,1,0:T(1,128)}), f32[4,1,2048]{2,1,0:T(1,128)S(1)}, u32[]{:S(2)}, u32[]{:S(2)}) async-start(f32[4,1,2048]{2,1,0:T(1,128)} %reshape.70), calls=%async_computation.2 | async-start | bytes 65536 | tf_op jit(solution)/shard_map/all_to_all | solution.py:204
Sparse Core Ops, SparseCore 0:
  427.7 21.8 reduce-scatter.1

commit v2 on v1

--- a/solution.py
+++ b/solution.py
@@ -12,8 +12,8 @@
 LAG = 2
 
 
-def chunk_of(count):
-    return max(k for k in range(1, 11) if count % k == 0)
+def chunk_of(count, most):
+    return max(k for k in range(1, most + 1) if count % k == 0)
 
 
 def split(x):
@@ -155,6 +155,298 @@
     return jnp.pad(cut, ((0, 0), (0, 0), (0, LANES - per * width)))
 
 
+def pair_kernel(n, cc, away, t_ref, ttail_ref, v_ref, vtail_ref, out_ref, held, stage, vbuf, far, away_v, vtail, far_tail,
+                acc, acc_away, got_away, got_pair, load_sem, stage_sem, v_sem, vt_sem, tp_send, tp_recv, vp_send,
+                vp_recv, z_send, z_recv, a_send, a_recv, back_sem, pair_sem):
+    occ_rows, c_count, j_count, _ = t_ref.shape
+    a_count, _, b_count, d_count = v_ref.shape
+    tail_tiles = ttail_ref.shape[1]
+    full = d_count // LANES
+    width = full * LANES
+    rows = n * occ_rows * j_count
+    cols = a_count * b_count
+    own_c = c_count // 2
+    mains = own_c // cc
+    chunks = mains + 1
+    line = n // 2
+
+    row = lax.axis_index("row")
+    z, y = lax.div(row, 2), lax.rem(row, 2)
+    pair = 2 * z + 1 - y
+    low_end, high_end = z == 0, z == line - 1
+    end = jnp.logical_or(low_end, high_end)
+    low_help, high_help = z == 1, z == line - 2
+    helper = jnp.logical_or(low_help, high_help)
+
+    def to(target):
+        return {"row": target}
+
+    def tiles(q):
+        if q < mains:
+            return pl.ds(q * full * cc, full * cc)
+        return pl.ds(mains * full * cc, tail_tiles)
+
+    def t_loads(q, side, target, sem):
+        if q == mains:
+            return [pltpu.make_async_copy(ttail_ref.at[side], target.at[tiles(q)], sem.at[q])]
+        return [
+            pltpu.make_async_copy(
+                t_ref.at[i, pl.ds(side * own_c + q * cc, cc), :, pl.ds(part * LANES, LANES)],
+                target.at[pl.ds(q * full * cc + part * cc, cc), pl.ds(i * j_count, j_count), :],
+                sem.at[q],
+            )
+            for i in range(occ_rows)
+            for part in range(full)
+        ]
+
+    def whole_wait(data, sem):
+        pltpu.make_async_copy(data, data, sem).wait()
+
+    def v_piece(q, side):
+        return v_ref.at[:, pl.ds(side * own_c + q * cc, cc), :, pl.ds(0, width)]
+
+    def v_load(q):
+        return pltpu.make_async_copy(v_piece(q, y), vbuf.at[q % 2], v_sem.at[q % 2])
+
+    own_vtail = pltpu.make_async_copy(vtail_ref.at[y], vtail, vt_sem)
+
+    def remote(src, dst, send, recv, target):
+        return pltpu.make_async_remote_copy(src_ref=src, dst_ref=dst, send_sem=send, recv_sem=recv,
+                                            device_id=to(target), device_id_type=MESH)
+
+    def t_to_pair(q):
+        return remote(stage.at[tiles(q)], held.at[row, tiles(q)], tp_send.at[q], tp_recv.at[q], pair)
+
+    def t_from_pair(q):
+        data = held.at[pair, tiles(q)]
+        return remote(data, data, tp_send.at[q], tp_recv.at[q], pair)
+
+    def v_to_pair(q):
+        if q == mains:
+            return remote(vtail_ref.at[1 - y], far_tail, vp_send.at[q], vp_recv.at[q], pair)
+        return remote(v_piece(q, 1 - y), far.at[q], vp_send.at[q], vp_recv.at[q], pair)
+
+    def along(q, step, way, arriving):
+        sign = 1 - 2 * way
+        start = z - sign * (step if arriving else step - 1)
+        data = held.at[pl.ds(2 * start, 2), tiles(q)]
+        return remote(data, data, z_send.at[q, step - 1, way], z_recv.at[q, step - 1, way], row + 2 * sign)
+
+    def sends(q, step, way):
+        last = line - 2 if q < away else line - 1
+        if way == 0:
+            return jnp.logical_and(z - (step - 1) >= 0, z + 1 <= last)
+        return jnp.logical_and(z + (step - 1) <= line - 1, z - 1 >= line - 1 - last)
+
+    def arrives(q, step, way):
+        last = line - 2 if q < away else line - 1
+        if way == 0:
+            return jnp.logical_and(z - step >= 0, z <= last)
+        return jnp.logical_and(z + step <= line - 1, z >= line - 1 - last)
+
+    def v_away(q, block, inner):
+        src = v_piece(q, y) if block == 0 else far.at[q]
+        return remote(src, away_v.at[q, block], a_send.at[q, block], a_recv.at[q, block], inner)
+
+    def v_arrived(q, block):
+        data = away_v.at[q, block]
+        return remote(data, data, a_send.at[q, block], a_recv.at[q, block], pair)
+
+    def back(outer):
+        return remote(acc_away, got_away, back_sem.at[0], back_sem.at[1], outer)
+
+    def exchange():
+        return remote(acc.at[1], got_pair, pair_sem.at[0], pair_sem.at[1], pair)
+
+    def on_ends(f):
+        pl.when(low_end)(lambda: f(row + 2))
+        pl.when(high_end)(lambda: f(row - 2))
+
+    def on_helpers(f):
+        pl.when(low_help)(lambda: f(row - 2))
+        pl.when(high_help)(lambda: f(row + 2))
+
+    def add_product(into, t, v_own, v_far):
+        t_high, t_low = split(t)
+        v_high, v_low = split(jnp.concatenate([v_own, v_far], axis=0))
+        dims = (((1,), (1,)), ((), ()))
+        both = lax.dot_general(t_high, jnp.concatenate([v_high, v_low], axis=0), dims,
+                               preferred_element_type=jnp.float32)
+        rest = lax.dot_general(t_low, v_high, dims, preferred_element_type=jnp.float32)
+        total = both[:, : 2 * cols] + both[:, 2 * cols:] + rest
+        into[0] += total[:, :cols]
+        into[1] += total[:, cols:]
+
+    def t_of(q, k):
+        return jnp.concatenate(
+            [held[:, q * full * cc + part * cc + k].reshape(rows, LANES) for part in range(full)], axis=1)
+
+    def compute(q):
+        v_to_pair(q).wait_recv()
+        if q == mains:
+            own_vtail.wait()
+
+            @pl.loop(0, tail_tiles)
+            def _(k):
+                add_product(acc, held[:, mains * full * cc + k].reshape(rows, LANES), vtail[k], far_tail[k])
+            return
+        v_load(q).wait()
+        if q < away:
+            on_ends(lambda inner: v_away(q, 1, inner).start())
+
+        def product():
+            @pl.loop(0, cc)
+            def _(k):
+                add_product(acc, t_of(q, k), vbuf[q % 2, :, k].reshape(cols, width), far[q, :, k].reshape(cols, width))
+
+        if q < away:
+            pl.when(jnp.logical_not(end))(product)
+        else:
+            product()
+        if q + 2 < mains:
+            v_load(q + 2).start()
+
+    def compute_away():
+        for q in range(away):
+            for block in range(2):
+                v_arrived(q, block).wait_recv()
+
+            @pl.loop(0, cc)
+            def _(k):
+                add_product(acc_away, t_of(q, k), away_v[q, 0, :, k].reshape(cols, width),
+                            away_v[q, 1, :, k].reshape(cols, width))
+
+    for q in range(chunks):
+        for copy in t_loads(q, 1 - y, stage, stage_sem) + t_loads(q, y, held.at[row], load_sem):
+            copy.start()
+    for q in range(min(2, mains)):
+        v_load(q).start()
+    own_vtail.start()
+    acc[...] = jnp.zeros_like(acc)
+    acc_away[...] = jnp.zeros_like(acc_away)
+
+    barrier = pltpu.get_barrier_semaphore()
+    pl.semaphore_signal(barrier, inc=1, device_id=to(pair), device_id_type=MESH)
+
+    @pl.when(z > 0)
+    def _():
+        pl.semaphore_signal(barrier, inc=1, device_id=to(row - 2), device_id_type=MESH)
+
+    @pl.when(z < line - 1)
+    def _():
+        pl.semaphore_signal(barrier, inc=1, device_id=to(row + 2), device_id_type=MESH)
+
+    pl.semaphore_wait(barrier, 1 + jnp.minimum(z, 1) + jnp.minimum(line - 1 - z, 1))
+
+    for q in range(chunks):
+        whole_wait(stage.at[tiles(q)], stage_sem.at[q])
+        t_to_pair(q).start()
+    for q in range(away):
+        on_ends(lambda inner, q=q: v_away(q, 0, inner).start())
+
+    help_turn = away - 1 + LAG * (line - 1) + 4
+    turns = chunks + LAG * (line - 1)
+    for turn in range(turns):
+        for q in ([0, 1, 2] if turn == 0 else [turn + 2]):
+            if q < chunks:
+                v_to_pair(q).start()
+        for step in range(1, line + 1):
+            q = turn - LAG * (step - 1)
+            if not 0 <= q < chunks:
+                continue
+            if step == 1:
+                whole_wait(held.at[row, tiles(q)], load_sem.at[q])
+                t_from_pair(q).wait_recv()
+            for way in range(2):
+                if step > 1:
+                    @pl.when(arrives(q, step - 1, way))
+                    def _():
+                        along(q, step - 1, way, True).wait_recv()
+                if step < line:
+                    @pl.when(sends(q, step, way))
+                    def _():
+                        along(q, step, way, False).start()
+            if step == line:
+                compute(q)
+        if away and turn == min(help_turn, turns - 1):
+            pl.when(helper)(compute_away)
+            on_helpers(lambda outer: back(outer).start())
+
+    if away:
+        @pl.when(end)
+        def _():
+            back(pair).wait_recv()
+            acc[...] += got_away[...]
+
+    exchange().start()
+    for q in range(chunks):
+        t_to_pair(q).wait_send()
+        v_to_pair(q).wait_send()
+        for way in range(2):
+            for step in range(1, line):
+                @pl.when(sends(q, step, way))
+                def _():
+                    along(q, step, way, False).wait_send()
+    if away:
+        for q in range(away):
+            for block in range(2):
+                on_ends(lambda inner, q=q, block=block: v_away(q, block, inner).wait_send())
+        on_helpers(lambda outer: back(outer).wait_send())
+    exchange().wait()
+    out_ref[...] = acc[0] + got_pair[...]
+
+
+def pair_ladder(n, amplitudes, integrals):
+    occ_rows, j_count, c_count, d_count = amplitudes.shape
+    a_count, b_count = integrals.shape[:2]
+    full = d_count // LANES
+    own_c = c_count // 2
+    t = jnp.transpose(amplitudes, (0, 2, 1, 3))
+    v = jnp.transpose(integrals, (0, 2, 1, 3))
+
+    def tails(x):
+        cut = jnp.transpose(x[..., full * LANES:], (1, 0, 2, 3)).reshape(2, own_c, -1, d_count - full * LANES)
+        return jax.vmap(lambda part: packed_tail(part, 0))(cut)
+
+    t_tail, v_tail = tails(t), tails(v)
+    cc = chunk_of(own_c, 5)
+    mains = own_c // cc
+    away = mains // 5
+    chunks, line = mains + 1, n // 2
+    tail_tiles = t_tail.shape[1]
+    held_rows = occ_rows * j_count
+    tiles = own_c * full + tail_tiles
+    rows, cols = n * held_rows, a_count * b_count
+    dma = pltpu.SemaphoreType.DMA
+    return pl.pallas_call(
+        functools.partial(pair_kernel, n, cc, away),
+        out_shape=jax.ShapeDtypeStruct((rows, cols), jnp.float32),
+        in_specs=[pl.BlockSpec(memory_space=pl.ANY)] * 4,
+        out_specs=pl.BlockSpec(memory_space=pltpu.VMEM),
+        scratch_shapes=[
+            pltpu.VMEM((n, tiles, held_rows, LANES), jnp.float32),
+            pltpu.VMEM((tiles, held_rows, LANES), jnp.float32),
+            pltpu.VMEM((2, a_count, cc, b_count, full * LANES), jnp.float32),
+            pltpu.VMEM((mains, a_count, cc, b_count, full * LANES), jnp.float32),
+            pltpu.VMEM((max(away, 1), 2, a_count, cc, b_count, full * LANES), jnp.float32),
+            pltpu.VMEM((tail_tiles, cols, LANES), jnp.float32),
+            pltpu.VMEM((tail_tiles, cols, LANES), jnp.float32),
+            pltpu.VMEM((2, rows, cols), jnp.float32),
+            pltpu.VMEM((2, rows, cols), jnp.float32),
+            pltpu.VMEM((2, rows, cols), jnp.float32),
+            pltpu.VMEM((rows, cols), jnp.float32),
+            dma((chunks,)), dma((chunks,)), dma((2,)), dma(()), dma((chunks,)), dma((chunks,)), dma((chunks,)),
+            dma((chunks,)), dma((chunks, line - 1, 2)), dma((chunks, line - 1, 2)), dma((max(away, 1), 2)),
+            dma((max(away, 1), 2)), dma((2,)), dma((2,)),
+        ],
+        compiler_params=pltpu.CompilerParams(
+            collective_id=1, has_side_effects=True, vmem_limit_bytes=58 * 2**20),
+        cost_estimate=pl.CostEstimate(
+            flops=6 * rows * cols * c_count * d_count,
+            bytes_accessed=4 * c_count * d_count * (rows + cols), transcendentals=0),
+    )(t, t_tail, v, v_tail)
+
+
 def partial_ladder(n, amplitudes, integrals):
     occ_rows, j_count, c_count, d_count = amplitudes.shape
     a_count, b_count = integrals.shape[:2]
@@ -165,7 +457,7 @@
         jnp.transpose(t[..., full * LANES:], (1, 0, 2, 3)).reshape(c_count, occ_rows * j_count, -1), 0)
     v_tail = packed_tail(
         jnp.transpose(v[..., full * LANES:], (1, 0, 2, 3)).reshape(c_count, a_count * b_count, -1), 0)
-    cc = chunk_of(c_count)
+    cc = chunk_of(c_count, 10)
     chunks = c_count // cc + 1
     tiles = c_count * full + t_tail.shape[0]
     rows, cols = n * occ_rows * j_count, a_count * b_count
@@ -198,7 +490,8 @@
     a_count = integrals.shape[0]
     b_count = integrals.shape[1]
     occupied = amplitudes.shape[1]
-    partial_value = partial_ladder(n, amplitudes, integrals).reshape(
+    ladder = pair_ladder if n >= 8 and amplitudes.shape[2] % 2 == 0 else partial_ladder
+    partial_value = ladder(n, amplitudes, integrals).reshape(
         n * amplitudes.shape[0], occupied, a_count, b_count)
     summed = lax.psum_scatter(partial_value, "col", scatter_dimension=0, tiled=True)
     moved = lax.all_to_all(

time: 483 us -> 417 us (0.86)
  Pallas kernels: 401 us -> 332 us
    pallas_call x1, Pallas kernels: 401 us -> 332 us  [pair_ladder(): pl.pallas_call(functools.partial(pair_kernel, n, cc, away), out_shape=jax...]
    unnamed x12 -> x13, local copies, waits for them, and re-layouts: 3.07 us -> 10.1 us
    transpose x4 -> x3, local copies, waits for them, and re-layouts: 14.2 us -> 8.54 us  [tails(): jnp.transpose(x[..., full * LANES:], (1, 0, 2, 3))]
where the time goes in v2:
time: 417 us; the launch traced here: 416 us
  Pallas kernels  332 us (80%)
  waiting for transfers between devices  32.4 us (8%)
  local copies, waits for them, and re-layouts  27.4 us (7%)
  between operations  13.6 us (3%)
  starting transfers between devices  8.78 us (2%)
    pallas_call x1, Pallas kernels, pair_ladder(): pl.pallas_call(functools.partial(pair_kernel, n, cc, away), out_shape=jax...  332 us
    reduce_scatter x1, waiting for transfers between devices, on_device(): lax.psum_scatter(partial_value, 'col', scatter_dimension=0, tiled=True)  22 us
    unnamed x13, local copies, waits for them, and re-layouts  10.1 us
    transpose x3, local copies, waits for them, and re-layouts, tails(): jnp.transpose(x[..., full * LANES:], (1, 0, 2, 3))  8.54 us
  transfers between devices with their start and end apart: 3, of which 3 were waited for; matrix products, arithmetic and copies ran while one was open for 0% of the time, Pallas kernels for 0%

profile of v2, /device:TPU:0, one launch (start us, length us, event | category | flops | bytes accessed | tf_op | source)
XLA Modules:
  0.0 416.2 jit_solution(7275512022123113891)
XLA Ops:
  6.5 0.0 reduce-scatter.2.cloned.1.call-start
  6.5 6.3 %slice_bitcast_fusion = f32[100,4,32,16]{3,2,0,1:T(8,128)} fusion(f32[4,100,32,400]{3,2,1,0:T(8,128)} %bitcast.36), kind=kLoop, calls=%fused_computation | loop fusion | bytes 1638400 | tf_op jit(solution)/shard_map/transpose | solution.py:408
  12.9 5.3 %copy.48 = f32[100,4,32,16]{2,1,3,0:T(4,128)S(1)} copy(f32[100,4,32,16]{3,2,0,1:T(8,128)} %slice_bitcast_fusion) | data formatting | bytes 1638400
  18.2 2.2 reshape.68
  20.4 1.2 pad.9.clone
  21.6 1.2 copy.36.vtail_ref
  22.9 1.5 slice_bitcast_fusion.1
  24.4 0.7 copy.31
  25.1 0.3 reshape.61
  25.4 0.6 copy.46
  26.0 0.1 pad.8.clone
  26.1 1.0 copy.35.ttail_ref
  27.0 0.0 copy-start.2
  27.0 0.0 copy-start.1
  27.0 0.0 copy-start
  27.0 331.5 %shard_map.55 = f32[256,128]{1,0:T(8,128)} custom-call(f32[2,100,16,400]{3,2,1,0:T(8,128)} %bitcast.39, f32[2,7,32,128]{3,2,1,0:T(8,128)} %copy.35.ttail_ref, f32[4,100,32,400]{3,2,1,0:T(8,128)} %bitcast.37, f32[2,7,128,128]{3,2,1,0:T(8,128)} %copy.36.vtail_ref), custom_call_target="tpu_custom_call" | custom-call | flops 7864320000 | bytes 61440000 | tf_op jit(solution)/shard_map/pallas_call | solution.py:421
  358.6 1.2 reshape.67
  359.7 0.8 copy.37
  360.6 0.0 reduce-scatter.2.cloned.1.call-update
  360.6 0.0 copy-done.2
  360.6 0.1 dynamic_slice.6
  360.7 22.0 %reduce-scatter.2.cloned.1.call-done = f32[4,16,4,32]{3,1,2,0:T(8,128)} async-done(((f32[16,16,4,32]{3,1,2,0:T(8,128)}), f32[4,16,4,32]{3,1,2,0:T(8,128)}) %reduce-scatter.2.cloned.1.call-update) | async-done | bytes 32784 | tf_op jit(solution)/shard_map/reduce_scatter | solution.py:496
  382.7 1.1 copy.38
  383.8 0.8 reshape.69
  384.6 5.5 %all-to-all-start = ((f32[8,1,1024]{2,1,0:T(1,128)}), f32[8,1,1024]{2,1,0:T(1,128)S(1)}, u32[]{:S(2)}, u32[]{:S(2)}) async-start(f32[8,1,1024]{2,1,0:T(1,128)} %reshape.69), calls=%async_computation.1 | async-start | bytes 65536 | tf_op jit(solution)/shard_map/all_to_all | solution.py:498
  390.1 0.1 broadcast_add_fusion
  390.2 0.0 copy-done.1
  390.2 0.1 dynamic_slice.7
  390.3 6.5 %all-to-all-done = f32[8,1,1024]{2,1,0:T(1,128)S(1)} async-done(((f32[8,1,1024]{2,1,0:T(1,128)}), f32[8,1,1024]{2,1,0:T(1,128)S(1)}, u32[]{:S(2)}, u32[]{:S(2)}) %all-to-all-start) | async-done | bytes 32800 | tf_op jit(solution)/shard_map/all_to_all | solution.py:498
  396.8 0.5 broadcast.41
  397.4 0.7 reduce
  398.1 0.2 reshape.70
  398.3 0.1 copy.39
  398.4 0.2 copy.40
  398.6 0.1 copy.41
  398.7 0.8 reshape.71
  399.5 3.3 all-to-all-start.1
  402.8 0.1 broadcast_subtract_fusion
  402.8 3.8 all-to-all-done.1
  406.7 0.7 reduce.1
  407.4 0.1 reshape.72
  407.6 0.1 copy.43
  407.7 0.0 copy-done
  407.7 1.0 fusion
  408.7 0.7 copy.45
  (1 shorter events, 0.0 us)
Async XLA Ops:
  6.5 376.2 %reduce-scatter.2.cloned.1.call-start = ((), (), s32[]{:S(2)}) async-start(), calls=%async_computation.3 | async-start | bytes 655360 | tf_op jit(solution)/shard_map/reduce_scatter | solution.py:496
  27.0 333.6 %copy-start.2 = (f32[32]{0:T(128)S(1)}, f32[32]{0:T(128)}, u32[]{:S(2)}) copy-start(f32[32]{0:T(128)} %param.9) | copy-start | bytes 388
  27.0 363.2 %copy-start.1 = (f32[16]{0:T(128)S(1)}, f32[16]{0:T(128)}, u32[]{:S(2)}) copy-start(f32[16]{0:T(128)} %param.8) | copy-start | bytes 196
  27.0 380.6 %copy-start = (f32[4,16,4,32]{3,2,1,0:T(4,128)S(1)}, f32[4,16,4,32]{3,2,1,0:T(4,128)}, u32[]{:S(2)}) copy-start(f32[4,16,4,32]{3,2,1,0:T(4,128)} %param.7) | copy-start | bytes 98308
  384.6 12.2 %all-to-all-start = ((f32[8,1,1024]{2,1,0:T(1,128)}), f32[8,1,1024]{2,1,0:T(1,128)S(1)}, u32[]{:S(2)}, u32[]{:S(2)}) async-start(f32[8,1,1024]{2,1,0:T(1,128)} %reshape.69), calls=%async_computation.1 | async-start | bytes 65536 | tf_op jit(solution)/shard_map/all_to_all | solution.py:498
  399.5 7.2 %all-to-all-start.1 = ((f32[4,1,2048]{2,1,0:T(1,128)}), f32[4,1,2048]{2,1,0:T(1,128)S(1)}, u32[]{:S(2)}, u32[]{:S(2)}) async-start(f32[4,1,2048]{2,1,0:T(1,128)} %reshape.71), calls=%async_computation.2 | async-start | bytes 65536 | tf_op jit(solution)/shard_map/all_to_all | solution.py:497
Sparse Core Ops, SparseCore 0:
  360.7 21.9 reduce-scatter.1

commit v3 on v2

--- a/solution.py
+++ b/solution.py
@@ -484,6 +484,18 @@
     )(t, t_tail, v, v_tail)
 
 
+def mirrored(product, rows, cols, occupied, a_count, b_count):
+    i_count = occupied // cols
+    pieces = lax.all_to_all(product, "col", split_axis=0, concat_axis=0, tiled=True)
+    summed = pieces.reshape(cols, -1, product.shape[1]).sum(axis=0)
+    blocks = summed.reshape(i_count, cols, i_count, a_count, rows, a_count).transpose(4, 1, 2, 0, 5, 3)
+    moved = lax.all_to_all(
+        blocks.reshape(rows * cols, -1), ("row", "col"), split_axis=0, concat_axis=0, tiled=True)
+    moved = moved.reshape(rows, cols, i_count, i_count, a_count, a_count).transpose(2, 1, 3, 4, 0, 5)
+    shape = (i_count, occupied, a_count, b_count)
+    return summed.reshape(shape) + moved.reshape(shape)
+
+
 def on_device(n, amplitudes, integrals, rest, occ_energy, vir_energy):
     row_index = lax.axis_index("row")
     col_index = lax.axis_index("col")
@@ -491,17 +503,8 @@
     b_count = integrals.shape[1]
     occupied = amplitudes.shape[1]
     ladder = pair_ladder if n >= 8 and amplitudes.shape[2] % 2 == 0 else partial_ladder
-    partial_value = ladder(n, amplitudes, integrals).reshape(
-        n * amplitudes.shape[0], occupied, a_count, b_count)
-    summed = lax.psum_scatter(partial_value, "col", scatter_dimension=0, tiled=True)
-    moved = lax.all_to_all(
-        lax.all_to_all(summed, "row", split_axis=3, concat_axis=2, tiled=True),
-        "col",
-        split_axis=1,
-        concat_axis=0,
-        tiled=True,
-    )
-    combined = summed + jnp.transpose(moved, (1, 0, 3, 2))
+    product = ladder(n, amplitudes, integrals)
+    combined = mirrored(product, n, lax.axis_size("col"), occupied, a_count, b_count)
     i_count = combined.shape[0]
     occ_local = lax.dynamic_slice_in_dim(occ_energy, col_index * i_count, i_count, 0)
     vir_local = lax.dynamic_slice_in_dim(vir_energy, row_index * a_count, a_count, 0)

time: 417 us -> 381 us (0.914)
  waiting for transfers between devices: 32.4 us -> 11.2 us
  between operations: 13.6 us -> 0.13 us
    reduce_scatter x1 -> x0, waiting for transfers between devices: 22 us -> none  [on_device(): lax.psum_scatter(partial_value, 'col', scatter_dimension=0, tiled=True)]
    unnamed x13 -> x9, local copies, waits for them, and re-layouts: 10.1 us -> 8.17 us
  transfers between devices with their start and end apart: 3 -> 2, of which waited for: 3 -> 2; matrix products, arithmetic and copies ran while one was open for 0% -> 0% of each run, Pallas kernels for 0% -> 0%
where the time goes in v3:
time: 381 us
  Pallas kernels  331 us (87%)
  local copies, waits for them, and re-layouts  29.1 us (8%)
  waiting for transfers between devices  11.2 us (3%)
  starting transfers between devices  7.61 us (2%)
    pallas_call x1, Pallas kernels, pair_ladder(): pl.pallas_call(functools.partial(pair_kernel, n, cc, away), out_shape=jax...  331 us
    transpose x3, local copies, waits for them, and re-layouts, tails(): jnp.transpose(x[..., full * LANES:], (1, 0, 2, 3))  8.54 us
    unnamed x9, local copies, waits for them, and re-layouts  8.17 us
  transfers between devices with their start and end apart: 2, of which 2 were waited for; matrix products, arithmetic and copies ran while one was open for 0% of the time, Pallas kernels for 0%

profile of v3, /device:TPU:0, one launch (start us, length us, event | category | flops | bytes accessed | tf_op | source)
XLA Modules:
  0.0 380.5 jit_solution(12059806912324147053)
XLA Ops:
  0.0 6.3 %slice_bitcast_fusion = f32[100,4,32,16]{3,2,0,1:T(8,128)} fusion(f32[4,100,32,400]{3,2,1,0:T(8,128)} %bitcast.27), kind=kLoop, calls=%fused_computation | loop fusion | bytes 1638400 | tf_op jit(solution)/shard_map/transpose | solution.py:408
  6.3 5.3 %copy.39 = f32[100,4,32,16]{2,1,3,0:T(4,128)S(1)} copy(f32[100,4,32,16]{3,2,0,1:T(8,128)} %slice_bitcast_fusion) | data formatting | bytes 1638400
  11.6 2.2 reshape.90
  13.9 1.2 pad.9.clone
  15.1 1.2 copy.30.vtail_ref
  16.3 1.5 slice_bitcast_fusion.1
  17.9 0.7 copy.25
  18.5 0.3 reshape.79
  18.8 0.6 copy.37
  19.5 0.1 pad.8.clone
  19.5 1.0 copy.29.ttail_ref
  20.5 0.0 copy-start.2
  20.5 0.0 copy-start.1
  20.5 331.5 %shard_map.55 = f32[256,128]{1,0:T(8,128)} custom-call(f32[2,100,16,400]{3,2,1,0:T(8,128)} %bitcast.30, f32[2,7,32,128]{3,2,1,0:T(8,128)} %copy.29.ttail_ref, f32[4,100,32,400]{3,2,1,0:T(8,128)} %bitcast.28, f32[2,7,128,128]{3,2,1,0:T(8,128)} %copy.30.vtail_ref), custom_call_target="tpu_custom_call" | custom-call | flops 7864320000 | bytes 61440000 | tf_op jit(solution)/shard_map/pallas_call | solution.py:421
  352.0 0.0 copy-start
  352.0 3.6 all-to-all-start
  355.7 0.0 copy-done.2
  355.7 0.1 dynamic_slice.6
  355.7 0.1 broadcast_add_fusion
  355.8 0.0 copy-done.1
  355.8 0.1 dynamic_slice.7
  355.9 4.2 %all-to-all-done = f32[4,64,128]{2,1,0:T(8,128)S(1)} async-done(((f32[4,64,128]{2,1,0:T(8,128)}), f32[4,64,128]{2,1,0:T(8,128)S(1)}, u32[]{:S(2)}, u32[]{:S(2)}) %all-to-all-start) | async-done | bytes 131104 | tf_op jit(solution)/shard_map/all_to_all | solution.py:489
  360.1 1.1 reshape.86
  361.2 3.2 copy.31
  364.4 1.7 all_to_all.16
  366.1 4.0 %all-to-all-start.1 = ((f32[32,1,256]{2,1,0:T(1,128)}), f32[32,1,256]{2,1,0:T(1,128)S(1)}, u32[]{:S(2)}, u32[]{:S(2)}) async-start(f32[32,1,256]{2,1,0:T(1,128)} %all_to_all.16), calls=%async_computation.1 | async-start | bytes 65536 | tf_op jit(solution)/shard_map/all_to_all | solution.py:492
  370.1 0.1 broadcast_subtract_fusion
  370.2 0.1 reshape.85
  370.3 7.1 %all-to-all-done.1 = f32[32,1,256]{2,1,0:T(1,128)S(1)} async-done(((f32[32,1,256]{2,1,0:T(1,128)}), f32[32,1,256]{2,1,0:T(1,128)S(1)}, u32[]{:S(2)}, u32[]{:S(2)}) %all-to-all-start.1) | async-done | bytes 32800 | tf_op jit(solution)/shard_map/all_to_all | solution.py:492
  377.3 0.1 reduce.1
  377.4 1.4 reshape.87
  378.8 0.6 copy.35
  379.4 0.3 reshape.89
  379.7 0.0 copy-done
  379.7 0.8 subtract_divide_fusion
  (1 shorter events, 0.0 us)
Async XLA Ops:
  20.5 335.1 %copy-start.2 = (f32[32]{0:T(128)S(1)}, f32[32]{0:T(128)}, u32[]{:S(2)}) copy-start(f32[32]{0:T(128)} %param.9) | copy-start | bytes 388
  20.5 335.3 %copy-start.1 = (f32[16]{0:T(128)S(1)}, f32[16]{0:T(128)}, u32[]{:S(2)}) copy-start(f32[16]{0:T(128)} %param.8) | copy-start | bytes 196
  352.0 27.8 %copy-start = (f32[4,16,4,32]{3,2,1,0:T(4,128)S(1)}, f32[4,16,4,32]{3,2,1,0:T(4,128)}, u32[]{:S(2)}) copy-start(f32[4,16,4,32]{3,2,1,0:T(4,128)} %param.7) | copy-start | bytes 98308
  352.0 8.1 %all-to-all-start = ((f32[4,64,128]{2,1,0:T(8,128)}), f32[4,64,128]{2,1,0:T(8,128)S(1)}, u32[]{:S(2)}, u32[]{:S(2)}) async-start(f32[4,64,128]{2,1,0:T(8,128)} %bitcast.35), calls=%async_computation | async-start | bytes 262144 | tf_op jit(solution)/shard_map/all_to_all | solution.py:489
  366.1 11.2 %all-to-all-start.1 = ((f32[32,1,256]{2,1,0:T(1,128)}), f32[32,1,256]{2,1,0:T(1,128)S(1)}, u32[]{:S(2)}, u32[]{:S(2)}) async-start(f32[32,1,256]{2,1,0:T(1,128)} %all_to_all.16), calls=%async_computation.1 | async-start | bytes 65536 | tf_op jit(solution)/shard_map/all_to_all | solution.py:492
